TPU v7x, 32 devices: a whole 2x2x4 slice. The times are simulated.
32 devices in a mesh: chan: 8 (over z, x), band: 4 (over y, core).
Axes of the slice: x: 2, y: 2, z: 4, core: 2. Of those that a mesh axis runs over, the one named last changes fastest.
Arguments:
- spectra: float32 [2, 32, 96, 1024], P(None, None, 'band', 'chan'), may hold values from -6 to 6
- taps: float32 [96, 16], replicated, may hold values from -2.5 to 2.5
Outputs:
- stacked: bfloat16 [8, 2, 1024, 1024], P('band', None, 'chan')
All inputs are finite; a program needn't handle non-finite values.
Results may differ from a plain program's by a relative error of at most 0.0057.
Values may be sent and summed in bfloat16 or wider, within the bound.
A program may use at most 192 MiB of HBM per device.

v0:
```python
from functools import partial

import jax
import jax.numpy as jnp
from jax import lax
from jax.sharding import PartitionSpec as P

TAPS = 16
SMOOTH = 5
BAND_BINS = 12


water_level = 0.1


def as_sent(shard):

    def short(part):
        return part.astype(jnp.bfloat16) if part.dtype == jnp.float32 else part

    return jax.tree.map(short, shard)


def shifted(shard, axis, by):
    devices = lax.axis_size(axis)
    return lax.ppermute(shard, axis, [(i, (i + by) % devices) for i in range(devices)])


def padded(shard, sides, width, wrap):
    for axis, dim in sides:
        devices, length = (lax.axis_size(axis), shard.shape[dim])
        up = [(i, (i + 1) % devices) for i in range(devices if wrap else devices - 1)]
        down = [(j, i) for i, j in up]
        last = lax.slice_in_dim(shard, length - width, length, axis=dim)
        first = lax.slice_in_dim(shard, 0, width, axis=dim)
        before = lax.ppermute(last, axis, up)
        after = lax.ppermute(first, axis, down)
        shard = jnp.concatenate([before, shard, after], axis=dim)
    return shard


def fan_filter(extended, coeffs, width):
    result = jnp.zeros(extended.shape[:-1] + (width,), jnp.float32)
    for tap_index in range(coeffs.shape[1]):
        result = (
            result + coeffs[:, tap_index][:, None] * extended[..., tap_index : tap_index + width]
        )
    return result


def whiten(filtered, amp_ext, local_bins):
    smoothed = jnp.zeros(filtered.shape[1:], jnp.float32)
    for offset in range(SMOOTH):
        smoothed = smoothed + amp_ext[:, offset : offset + local_bins, :]
    smoothed = smoothed / SMOOTH
    return (filtered / (smoothed + water_level)[None]).astype(jnp.bfloat16)


def arrange(whitened, band_count):
    shaped = whitened.reshape(2, whitened.shape[1], band_count, BAND_BINS, whitened.shape[3])
    shaped = shaped.transpose(2, 0, 1, 3, 4)
    return shaped.reshape(band_count, 2 * whitened.shape[1] * BAND_BINS, whitened.shape[3])


def partner(whitened):
    return jnp.concatenate([-whitened[1:2], whitened[0:1]], axis=0)


def send_back(tile_value, amount):
    return jax.tree.map(
        lambda part, own: part.astype(own.dtype),
        shifted(as_sent(tile_value), "chan", -amount),
        tile_value,
    )


def body(spectra, taps):
    half_taps = TAPS // 2
    reach = SMOOTH // 2
    local_bins = spectra.shape[2]
    local_chan = spectra.shape[3]
    anchor = lax.axis_index("band") * local_bins
    padded_taps = jnp.pad(taps, ((reach, reach), (0, 0)))
    coeffs = lax.dynamic_slice_in_dim(padded_taps, anchor + reach, local_bins, 0)
    extended = padded(spectra, (("chan", 3),), half_taps, True)
    filtered = fan_filter(extended, coeffs, local_chan)
    amplitude = jnp.sqrt(filtered[0] * filtered[0] + filtered[1] * filtered[1])
    amp_ext = padded(amplitude, (("band", 1),), reach, False)
    whitened = whiten(filtered, amp_ext, local_bins)
    band_count = local_bins // BAND_BINS
    features = arrange(whitened, band_count)
    scale_factor = 1.0 / (whitened.shape[1] * BAND_BINS)

    def cross(remote):
        right = arrange(remote, band_count)
        turned = arrange(partner(remote), band_count)
        real_part = jnp.einsum("bki,bkj->bij", features, right, preferred_element_type=jnp.float32)
        imag_part = jnp.einsum("bki,bkj->bij", features, turned, preferred_element_type=jnp.float32)
        return (jnp.stack([real_part, imag_part], axis=1) * scale_factor).astype(jnp.bfloat16)

    cycle_size = lax.axis_size("chan")
    halfway = cycle_size // 2
    own_index = lax.axis_index("chan")
    tile_shape = (band_count, 2, local_chan, local_chan)
    near_tiles = jnp.zeros((halfway + 1,) + tile_shape, jnp.bfloat16)
    outgoing = jnp.zeros((halfway,) + tile_shape, jnp.bfloat16)

    def advance(step_index, carry):
        current, near_tiles, outgoing = carry
        tile_value = cross(current)
        near_tiles = lax.dynamic_update_index_in_dim(near_tiles, tile_value, step_index, 0)
        mirror = jnp.stack([tile_value[:, 0], -tile_value[:, 1]], axis=1).transpose(0, 1, 3, 2)
        outgoing = lax.dynamic_update_index_in_dim(outgoing, mirror, step_index, 0)
        current = shifted(current, "chan", 1)
        return (current, near_tiles, outgoing)

    current, near_tiles, outgoing = lax.fori_loop(
        0, halfway, advance, (whitened, near_tiles, outgoing)
    )
    final_tile = cross(current)
    near_tiles = lax.dynamic_update_index_in_dim(near_tiles, final_tile, halfway, 0)
    branches = [partial(send_back, amount=amount) for amount in range(halfway)]

    def deliver(step_index, returned):
        tile_value = lax.dynamic_index_in_dim(outgoing, step_index, 0, keepdims=False)
        arrived = lax.switch(step_index, branches, tile_value)
        return lax.dynamic_update_index_in_dim(returned, arrived, step_index, 0)

    returned = lax.fori_loop(1, halfway, deliver, jnp.zeros((halfway,) + tile_shape, jnp.bfloat16))
    offsets = (own_index - jnp.arange(cycle_size, dtype=jnp.int32)) % cycle_size
    chosen = jnp.take(near_tiles, jnp.minimum(offsets, halfway), axis=0)
    far_slot = jnp.clip(cycle_size - offsets, 0, halfway - 1)
    mirrored = jnp.take(returned, far_slot, axis=0)
    blocks = jnp.where((offsets <= halfway)[:, None, None, None, None], chosen, mirrored)
    return blocks.transpose(1, 2, 3, 0, 4).reshape(
        band_count, 2, local_chan, cycle_size * local_chan
    )


def solution(mesh):
    placed = (P(None, None, "band", "chan"), P())
    return jax.shard_map(
        body, mesh=mesh, in_specs=placed, out_specs=P("band", None, "chan", None), check_vma=False
    )
```

profile of v0, /device:TPU:0, one launch (start us, length us, event | category | flops | bytes accessed | tf_op | source)
XLA Modules:
  0.0 111.4 jit_solution(194734860702655191)
XLA Ops:
  0.0 1.7 %fusion.86 = (f32[2,32,24,8]{3,2,1,0:T(8,128)S(1)}, f32[2,32,24,8]{3,2,1,0:T(8,128)S(1)}) fusion(f32[2,32,24,128]{3,2,1,0:T(8,128)} %param.10), kind=kLoop, calls=%fused_computation.176 | loop fusion | bytes 196608 | tf_op jit(solution)/shard_map/slice | solution.py:34
  2.0 3.0 %collective-permute-start.5 = (f32[2,32,24,8]{1,3,2,0:T(8,128)S(1)}, f32[2,32,24,8]{1,3,2,0:T(8,128)S(1)}, u32[]{:S(2)}, u32[]{:S(2)}) collective-permute-start(f32[2,32,24,8]{1,3,2,0:T(8,128)S(1)} %copy.96), channel_id=1, source_target_pairs={{0,4},{4,8},{8,12},{12,16},{16,20},{20,24},{24,28},{28,0},{1,5},{5... | collective-permute-start | bytes 147464 | tf_op jit(solution)/shard_map/ppermute | solution.py:36
  5.2 3.1 %collective-permute-start.6 = (f32[2,32,24,8]{1,3,2,0:T(8,128)S(1)}, f32[2,32,24,8]{1,3,2,0:T(8,128)S(1)}, u32[]{:S(2)}, u32[]{:S(2)}) collective-permute-start(f32[2,32,24,8]{1,3,2,0:T(8,128)S(1)} %copy.97), channel_id=1, source_target_pairs={{4,0},{8,4},{12,8},{16,12},{20,16},{24,20},{28,24},{0,28},{5,1},{9... | collective-permute-start | bytes 147464 | tf_op jit(solution)/shard_map/ppermute | solution.py:37
  8.7 4.6 %collective-permute-done.5 = f32[2,32,24,8]{1,3,2,0:T(8,128)S(1)} collective-permute-done((f32[2,32,24,8]{1,3,2,0:T(8,128)S(1)}, f32[2,32,24,8]{1,3,2,0:T(8,128)S(1)}, u32[]{:S(2)}, u32[]{:S(2)}) %collective-permute-start.5) | collective-permute-done | bytes 49184 | tf_op jit(solution)/shard_map/ppermute | solution.py:36
  13.6 2.2 %collective-permute-done.6 = f32[2,32,24,8]{1,3,2,0:T(8,128)S(1)} collective-permute-done((f32[2,32,24,8]{1,3,2,0:T(8,128)S(1)}, f32[2,32,24,8]{1,3,2,0:T(8,128)S(1)}, u32[]{:S(2)}, u32[]{:S(2)}) %collective-permute-start.6) | collective-permute-done | bytes 49184 | tf_op jit(solution)/shard_map/ppermute | solution.py:37
  16.1 6.6 %fusion.9 = f32[2,32,24,128]{3,1,2,0:T(8,128)S(1)} fusion(f32[2,32,24,128]{3,1,2,0:T(8,128)S(1)} %copy.71, f32[2,32,24,8]{3,1,2,0:T(8,128)S(1)} %copy.75, f32[2,32,24,8]{3,1,2,0:T(8,128)S(1)} %copy.70, f32[24]{0:T(128)S(1)} %get-tuple-element.317, f32[24]{0:T(128)S(1)} %get-tuple-element.303, f32[24]{0:T(128)S(1)} %get-tuple-element.304, ...), kind=kLoop, calls=%fused_computation.53 | loop fusion | flops 9043968 | bytes 1672704 | tf_op jit(solution)/shard_map/add | solution.py:46
  22.8 1.3 %collective-permute-start.7 = (f32[32,2,128]{2,0,1:T(8,128)S(1)}, f32[32,2,128]{2,0,1:T(8,128)S(1)}, u32[]{:S(2)}, u32[]{:S(2)}) collective-permute-start(f32[32,2,128]{2,0,1:T(8,128)S(1)} %get-tuple-element.300), channel_id=1, source_target_pairs={{0,1},{1,2},{2,3},{4,5},{5,6},{6,7},{8,9},{9,10},{10,11},{12,13},{... | collective-permute-start | bytes 98312 | tf_op jit(solution)/shard_map/ppermute | solution.py:36
  24.1 1.3 %collective-permute-start.8 = (f32[32,2,128]{2,0,1:T(8,128)S(1)}, f32[32,2,128]{2,0,1:T(8,128)S(1)}, u32[]{:S(2)}, u32[]{:S(2)}) collective-permute-start(f32[32,2,128]{2,0,1:T(8,128)S(1)} %get-tuple-element.301), channel_id=1, source_target_pairs={{1,0},{2,1},{3,2},{5,4},{6,5},{7,6},{9,8},{10,9},{11,10},{13,12},{... | collective-permute-start | bytes 98312 | tf_op jit(solution)/shard_map/ppermute | solution.py:37
  25.4 3.5 %collective-permute-done.8 = f32[32,2,128]{2,0,1:T(8,128)S(1)} collective-permute-done((f32[32,2,128]{2,0,1:T(8,128)S(1)}, f32[32,2,128]{2,0,1:T(8,128)S(1)}, u32[]{:S(2)}, u32[]{:S(2)}) %collective-permute-start.8) | collective-permute-done | bytes 32800 | tf_op jit(solution)/shard_map/ppermute | solution.py:37
  29.9 54.8 %while.32 = (s32[]{:T(128)}, bf16[2,32,24,128]{3,1,2,0:T(8,128)(2,1)S(1)}, bf16[5,2,2,128,128]{4,3,2,1,0:T(8,128)(2,1)S(1)}, bf16[4,2,2,128,128]{4,3,2,1,0:T(8,1...) while((s32[]{:T(128)}, bf16[2,32,24,128]{3,1,2,0:T(8,128)(2,1)S(1)}, ...), condition=%wide.region_1.2_spmd, body=%wide.region_0.1_spmd.sunk | while | flops 101449728 | bytes 9175161 | solution.py:117
  32.2 10.8 %collective-permute-done.4 = bf16[2,32,24,128]{3,1,2,0:T(8,128)(2,1)S(1)} collective-permute-done((bf16[2,32,24,128]{3,1,2,0:T(8,128)(2,1)S(1)}, bf16[2,32,24,128]{3,1,2,0:T(8,128)(2,1)S(1)}, u32[]{:S(2)}, u32[]{:S(2)}) %collective-permute-start.4) | collective-permute-done | bytes 393248 | tf_op jit(solution)/shard_map/while/body/eval_jaxpr/ppermute | solution.py:26
  44.9 12.3 %collective-permute-done.4 = bf16[2,32,24,128]{3,1,2,0:T(8,128)(2,1)S(1)} collective-permute-done((bf16[2,32,24,128]{3,1,2,0:T(8,128)(2,1)S(1)}, bf16[2,32,24,128]{3,1,2,0:T(8,128)(2,1)S(1)}, u32[]{:S(2)}, u32[]{:S(2)}) %collective-permute-start.4) | collective-permute-done | bytes 393248 | tf_op jit(solution)/shard_map/while/body/eval_jaxpr/ppermute | solution.py:26
  59.2 12.2 %collective-permute-done.4 = bf16[2,32,24,128]{3,1,2,0:T(8,128)(2,1)S(1)} collective-permute-done((bf16[2,32,24,128]{3,1,2,0:T(8,128)(2,1)S(1)}, bf16[2,32,24,128]{3,1,2,0:T(8,128)(2,1)S(1)}, u32[]{:S(2)}, u32[]{:S(2)}) %collective-permute-start.4) | collective-permute-done | bytes 393248 | tf_op jit(solution)/shard_map/while/body/eval_jaxpr/ppermute | solution.py:26
  73.3 11.4 %collective-permute-done.4 = bf16[2,32,24,128]{3,1,2,0:T(8,128)(2,1)S(1)} collective-permute-done((bf16[2,32,24,128]{3,1,2,0:T(8,128)(2,1)S(1)}, bf16[2,32,24,128]{3,1,2,0:T(8,128)(2,1)S(1)}, u32[]{:S(2)}, u32[]{:S(2)}) %collective-permute-start.4) | collective-permute-done | bytes 393248 | tf_op jit(solution)/shard_map/while/body/eval_jaxpr/ppermute | solution.py:26
  86.4 19.3 %while.33 = (s32[]{:T(128)}, bf16[4,2,2,128,128]{4,3,2,1,0:T(8,128)(2,1)S(1)}, bf16[4,2,2,128,128]{4,3,2,1,0:T(8,128)(2,1)S(1)}, s32[]{:T(128)}, s32[]{:T(128)}, /*index=5*/s32[]{:T(128)}, s32[]{:T(128)}) while((s32[]{:T(128)}, bf16[4,2,2,128,128]{4,3,2,1,0:T(8,128)(2,1)S(1)}, bf16[4,2,2,128,128]{4,3,2,1,0:T(8,128)(2,1)S(1)}, s32[]{:T(128)}, ...), condition=%wide.region_7.8_spmd, body=%wide.region_2.7_spmd.sunk | while | flops 6 | bytes 1048783 | solution.py:129
  86.4 5.2 %conditional.2 = (bf16[1,2,2,128,128]{4,3,2,1,0:T(8,128)(2,1)}) conditional(s32[]{:T(128)} %clamp.25, (bf16[4,2,2,128,128]{4,3,2,1,0:T(8,128)(2,1)S(1)}, s32[]{:T(128)}) %tuple.123, (bf16[4,2,2,128,128]{4,3,2,1,0:T(8,128)(2,1)S(1)}, s32[]{:T(128)}) %tuple.123, (bf16[4,2,2,128,128]{4,3,2,1,0:T(8,128)(2,1)S(1)}, ...), branch_computations={%region_3.3_spmd, %region_4.4_spmd, %region_5.5_spmd, %region_6.6_... | conditional | bytes 786484 | solution.py:126
  86.5 5.1 %collective-permute-done.1 = bf16[2,2,128,128]{3,2,1,0:T(8,128)(2,1)} collective-permute-done((bf16[2,2,128,128]{3,2,1,0:T(8,128)(2,1)S(1)}, bf16[2,2,128,128]{3,2,1,0:T(8,128)(2,1)}, u32[]{:S(2)}, u32[]{:S(2)}) %collective-permute-start.1) | collective-permute-done | bytes 131104 | tf_op jit(solution)/shard_map/while/body/eval_jaxpr/cond/branch_1_fun/ppermute | solution.py:26
  92.5 5.2 %conditional.2 = (bf16[1,2,2,128,128]{4,3,2,1,0:T(8,128)(2,1)}) conditional(s32[]{:T(128)} %clamp.25, (bf16[4,2,2,128,128]{4,3,2,1,0:T(8,128)(2,1)S(1)}, s32[]{:T(128)}) %tuple.123, (bf16[4,2,2,128,128]{4,3,2,1,0:T(8,128)(2,1)S(1)}, s32[]{:T(128)}) %tuple.123, (bf16[4,2,2,128,128]{4,3,2,1,0:T(8,128)(2,1)S(1)}, ...), branch_computations={%region_3.3_spmd, %region_4.4_spmd, %region_5.5_spmd, %region_6.6_... | conditional | bytes 786484 | solution.py:126
  92.6 5.1 %collective-permute-done.2 = bf16[2,2,128,128]{3,2,1,0:T(8,128)(2,1)} collective-permute-done((bf16[2,2,128,128]{3,2,1,0:T(8,128)(2,1)S(1)}, bf16[2,2,128,128]{3,2,1,0:T(8,128)(2,1)}, u32[]{:S(2)}, u32[]{:S(2)}) %collective-permute-start.2) | collective-permute-done | bytes 131104 | tf_op jit(solution)/shard_map/while/body/eval_jaxpr/cond/branch_2_fun/ppermute | solution.py:26
  98.6 6.1 %conditional.2 = (bf16[1,2,2,128,128]{4,3,2,1,0:T(8,128)(2,1)}) conditional(s32[]{:T(128)} %clamp.25, (bf16[4,2,2,128,128]{4,3,2,1,0:T(8,128)(2,1)S(1)}, s32[]{:T(128)}) %tuple.123, (bf16[4,2,2,128,128]{4,3,2,1,0:T(8,128)(2,1)S(1)}, s32[]{:T(128)}) %tuple.123, (bf16[4,2,2,128,128]{4,3,2,1,0:T(8,128)(2,1)S(1)}, ...), branch_computations={%region_3.3_spmd, %region_4.4_spmd, %region_5.5_spmd, %region_6.6_... | conditional | bytes 786484 | solution.py:126
  98.7 1.3 %collective-permute-start.3 = (bf16[2,2,128,128]{3,2,1,0:T(8,128)(2,1)S(1)}, bf16[2,2,128,128]{3,2,1,0:T(8,128)(2,1)}, u32[]{:S(2)}, u32[]{:S(2)}) collective-permute-start(bf16[2,2,128,128]{3,2,1,0:T(8,128)(2,1)S(1)} %dynamic-slice_bitcast_fusion.3), channel_id=1, source_target_pairs={{0,20},{4,24},{8,28},{12,0},{16,4},{20,8},{24,12},{28,16},{1,21},{... | collective-permute-start | bytes 393224 | tf_op jit(solution)/shard_map/while/body/eval_jaxpr/cond/branch_3_fun/ppermute | solution.py:26
  100.0 4.7 %collective-permute-done.3 = bf16[2,2,128,128]{3,2,1,0:T(8,128)(2,1)} collective-permute-done((bf16[2,2,128,128]{3,2,1,0:T(8,128)(2,1)S(1)}, bf16[2,2,128,128]{3,2,1,0:T(8,128)(2,1)}, u32[]{:S(2)}, u32[]{:S(2)}) %collective-permute-start.3) | collective-permute-done | bytes 131104 | tf_op jit(solution)/shard_map/while/body/eval_jaxpr/cond/branch_3_fun/ppermute | solution.py:26
  108.4 1.6 %copy.88 = bf16[2,2,128,8,128]{2,4,3,1,0:T(8,128)(2,1)S(1)} copy(bf16[2,2,128,8,128]{4,2,1,0,3:T(8,128)(2,1)} %select_bitcast_fusion) | data formatting | bytes 2097152 | tf_op jit(solution)/shard_map/jit(_where)/select_n | solution.py:134
  110.0 1.3 %copy.89 = bf16[2,2,128,1024]{3,2,1,0:T(8,128)(2,1)} copy(bf16[2,2,128,1024]{2,3,1,0:T(8,128)(2,1)S(1)} %bitcast.122) | data formatting | bytes 2097152 | tf_op jit(solution)/shard_map/reshape | solution.py:135
  (96 shorter events, 17.5 us)
Async XLA Ops:
  1.7 6.6 %copy-start.1 = (f32[96,16]{0,1:T(8,128)S(1)}, f32[96,16]{0,1:T(8,128)}, u32[]{:S(2)}) copy-start(f32[96,16]{0,1:T(8,128)} %param.11) | copy-start | bytes 18436
  1.7 6.8 %copy-start = (f32[2,32,24,128]{3,2,1,0:T(8,128)S(1)}, f32[2,32,24,128]{3,2,1,0:T(8,128)}, u32[]{:S(2)}) copy-start(f32[2,32,24,128]{3,2,1,0:T(8,128)} %param.10) | copy-start | bytes 2359300
  2.0 11.3 %collective-permute-start.5 = (f32[2,32,24,8]{1,3,2,0:T(8,128)S(1)}, f32[2,32,24,8]{1,3,2,0:T(8,128)S(1)}, u32[]{:S(2)}, u32[]{:S(2)}) collective-permute-start(f32[2,32,24,8]{1,3,2,0:T(8,128)S(1)} %copy.96), channel_id=1, source_target_pairs={{0,4},{4,8},{8,12},{12,16},{16,20},{20,24},{24,28},{28,0},{1,5},{5... | collective-permute-start | bytes 147464 | tf_op jit(solution)/shard_map/ppermute | solution.py:36
  5.2 10.6 %collective-permute-start.6 = (f32[2,32,24,8]{1,3,2,0:T(8,128)S(1)}, f32[2,32,24,8]{1,3,2,0:T(8,128)S(1)}, u32[]{:S(2)}, u32[]{:S(2)}) collective-permute-start(f32[2,32,24,8]{1,3,2,0:T(8,128)S(1)} %copy.97), channel_id=1, source_target_pairs={{4,0},{8,4},{12,8},{16,12},{20,16},{24,20},{28,24},{0,28},{5,1},{9... | collective-permute-start | bytes 147464 | tf_op jit(solution)/shard_map/ppermute | solution.py:37
  22.8 2.6 %collective-permute-start.7 = (f32[32,2,128]{2,0,1:T(8,128)S(1)}, f32[32,2,128]{2,0,1:T(8,128)S(1)}, u32[]{:S(2)}, u32[]{:S(2)}) collective-permute-start(f32[32,2,128]{2,0,1:T(8,128)S(1)} %get-tuple-element.300), channel_id=1, source_target_pairs={{0,1},{1,2},{2,3},{4,5},{5,6},{6,7},{8,9},{9,10},{10,11},{12,13},{... | collective-permute-start | bytes 98312 | tf_op jit(solution)/shard_map/ppermute | solution.py:36
  24.1 4.9 %collective-permute-start.8 = (f32[32,2,128]{2,0,1:T(8,128)S(1)}, f32[32,2,128]{2,0,1:T(8,128)S(1)}, u32[]{:S(2)}, u32[]{:S(2)}) collective-permute-start(f32[32,2,128]{2,0,1:T(8,128)S(1)} %get-tuple-element.301), channel_id=1, source_target_pairs={{1,0},{2,1},{3,2},{5,4},{6,5},{7,6},{9,8},{10,9},{11,10},{13,12},{... | collective-permute-start | bytes 98312 | tf_op jit(solution)/shard_map/ppermute | solution.py:37
  30.0 13.0 %collective-permute-start.4 = (bf16[2,32,24,128]{3,1,2,0:T(8,128)(2,1)S(1)}, bf16[2,32,24,128]{3,1,2,0:T(8,128)(2,1)S(1)}, u32[]{:S(2)}, u32[]{:S(2)}) collective-permute-start(bf16[2,32,24,128]{3,1,2,0:T(8,128)(2,1)S(1)} %copy.136), channel_id=1, source_target_pairs={{0,4},{4,8},{8,12},{12,16},{16,20},{20,24},{24,28},{28,0},{1,5},{5... | collective-permute-start | bytes 1179656 | tf_op jit(solution)/shard_map/while/body/eval_jaxpr/ppermute | solution.py:26
  43.0 14.2 %collective-permute-start.4 = (bf16[2,32,24,128]{3,1,2,0:T(8,128)(2,1)S(1)}, bf16[2,32,24,128]{3,1,2,0:T(8,128)(2,1)S(1)}, u32[]{:S(2)}, u32[]{:S(2)}) collective-permute-start(bf16[2,32,24,128]{3,1,2,0:T(8,128)(2,1)S(1)} %copy.136), channel_id=1, source_target_pairs={{0,4},{4,8},{8,12},{12,16},{16,20},{20,24},{24,28},{28,0},{1,5},{5... | collective-permute-start | bytes 1179656 | tf_op jit(solution)/shard_map/while/body/eval_jaxpr/ppermute | solution.py:26
  57.3 14.1 %collective-permute-start.4 = (bf16[2,32,24,128]{3,1,2,0:T(8,128)(2,1)S(1)}, bf16[2,32,24,128]{3,1,2,0:T(8,128)(2,1)S(1)}, u32[]{:S(2)}, u32[]{:S(2)}) collective-permute-start(bf16[2,32,24,128]{3,1,2,0:T(8,128)(2,1)S(1)} %copy.136), channel_id=1, source_target_pairs={{0,4},{4,8},{8,12},{12,16},{16,20},{20,24},{24,28},{28,0},{1,5},{5... | collective-permute-start | bytes 1179656 | tf_op jit(solution)/shard_map/while/body/eval_jaxpr/ppermute | solution.py:26
  71.4 13.3 %collective-permute-start.4 = (bf16[2,32,24,128]{3,1,2,0:T(8,128)(2,1)S(1)}, bf16[2,32,24,128]{3,1,2,0:T(8,128)(2,1)S(1)}, u32[]{:S(2)}, u32[]{:S(2)}) collective-permute-start(bf16[2,32,24,128]{3,1,2,0:T(8,128)(2,1)S(1)} %copy.136), channel_id=1, source_target_pairs={{0,4},{4,8},{8,12},{12,16},{16,20},{20,24},{24,28},{28,0},{1,5},{5... | collective-permute-start | bytes 1179656 | tf_op jit(solution)/shard_map/while/body/eval_jaxpr/ppermute | solution.py:26
  86.4 5.1 %collective-permute-start.1 = (bf16[2,2,128,128]{3,2,1,0:T(8,128)(2,1)S(1)}, bf16[2,2,128,128]{3,2,1,0:T(8,128)(2,1)}, u32[]{:S(2)}, u32[]{:S(2)}) collective-permute-start(bf16[2,2,128,128]{3,2,1,0:T(8,128)(2,1)S(1)} %dynamic-slice_bitcast_fusion.1), channel_id=1, source_target_pairs={{0,28},{4,0},{8,4},{12,8},{16,12},{20,16},{24,20},{28,24},{1,29},{... | collective-permute-start | bytes 393224 | tf_op jit(solution)/shard_map/while/body/eval_jaxpr/cond/branch_1_fun/ppermute | solution.py:26
  92.5 5.1 %collective-permute-start.2 = (bf16[2,2,128,128]{3,2,1,0:T(8,128)(2,1)S(1)}, bf16[2,2,128,128]{3,2,1,0:T(8,128)(2,1)}, u32[]{:S(2)}, u32[]{:S(2)}) collective-permute-start(bf16[2,2,128,128]{3,2,1,0:T(8,128)(2,1)S(1)} %dynamic-slice_bitcast_fusion.2), channel_id=1, source_target_pairs={{0,24},{4,28},{8,0},{12,4},{16,8},{20,12},{24,16},{28,20},{1,25},{... | collective-permute-start | bytes 393224 | tf_op jit(solution)/shard_map/while/body/eval_jaxpr/cond/branch_2_fun/ppermute | solution.py:26
  98.7 6.0 %collective-permute-start.3 = (bf16[2,2,128,128]{3,2,1,0:T(8,128)(2,1)S(1)}, bf16[2,2,128,128]{3,2,1,0:T(8,128)(2,1)}, u32[]{:S(2)}, u32[]{:S(2)}) collective-permute-start(bf16[2,2,128,128]{3,2,1,0:T(8,128)(2,1)S(1)} %dynamic-slice_bitcast_fusion.3), channel_id=1, source_target_pairs={{0,20},{4,24},{8,28},{12,0},{16,4},{20,8},{24,12},{28,16},{1,21},{... | collective-permute-start | bytes 393224 | tf_op jit(solution)/shard_map/while/body/eval_jaxpr/cond/branch_3_fun/ppermute | solution.py:26
where the time goes:
time: 112 us; the launch traced here: 111 us
  waiting for transfers between devices  71.9 us (64%)
  local copies, waits for them, and re-layouts  15.9 us (14%)
  starting transfers between devices  10.6 us (9%)
  other arithmetic  9.1 us (8%)
  matrix products  3.08 us (3%)
    ppermute x7, waiting for transfers between devices, shifted(): lax.ppermute(shard, axis, [(i, (i + by) % devices) for i in range(devices)])  61.6 us
    add x1, other arithmetic, fan_filter(): result + coeffs[:, tap_index][:, None] * extended[..., tap_index:tap_inde...  6.57 us
    ppermute x2, waiting for transfers between devices, padded(): after = lax.ppermute(first, axis, down)  5.71 us
    ppermute x2, waiting for transfers between devices, padded(): before = lax.ppermute(last, axis, up)  4.6 us
    transpose x11, local copies, waits for them, and re-layouts, arrange(): shaped = shaped.transpose(2, 0, 1, 3, 4)  4.48 us
    ppermute x2, starting transfers between devices, padded(): after = lax.ppermute(first, axis, down)  4.36 us
    ppermute x2, starting transfers between devices, padded(): before = lax.ppermute(last, axis, up)  4.25 us
    dynamic_update_slice x3, local copies, waits for them, and re-layouts, deliver(): return lax.dynamic_update_index_in_dim(returned, arrived, step_index, 0)  2.77 us
  transfers between devices with their start and end apart: 11, of which 10 were waited for; matrix products, arithmetic and copies ran while one was open for 7% of the time, Pallas kernels for 0%

commit v1 on v0

v1 whole, which is shorter than its diff:
```python
from functools import partial

import jax
import jax.numpy as jnp
from jax import lax
from jax.experimental import pallas as pl
from jax.experimental.pallas import tpu as pltpu
from jax.sharding import PartitionSpec as P

SMOOTH = 5
BAND_BINS = 12
WATER = 0.1
MESH = pl.DeviceIdType.MESH
F32, BF16 = jnp.float32, jnp.bfloat16


def rolled(value, by, axis):
    if isinstance(by, int):
        by = by % value.shape[axis]
        if by == 0:
            return value
    return pltpu.roll(value, by, axis)


def kernel(
    n, m, x_ref, taps_ref, out_ref, coef, edge_out, edge_in, filt, amp, rim_out, rim_in, held, left,
    edge_send, edge_recv, rim_send, rim_recv, block_send, block_recv,
):
    windows, bins, lanes = x_ref.shape[1:]
    tap_count = taps_ref.shape[1]
    half = tap_count // 2
    per = lanes // half
    groups = windows // 4
    depth = held.shape[2]
    piece = depth // 2
    part = piece // 2
    me = lax.axis_index("chan")
    group = lax.axis_index("band")
    chan_up, chan_down = lax.rem(me + 1, n), lax.rem(me + n - 1, n)
    band_up, band_down = lax.rem(group + 1, m), lax.rem(group + m - 1, m)
    odd = lax.rem(me, 2)
    pos = (1 - odd) * lax.div(me, 2) + odd * (n - 1 - lax.div(me, 2))

    def place(p):
        far = lax.div(p, (n + 1) // 2)
        return (1 - far) * 2 * p + far * (2 * (n - 1 - p) + 1)

    ring = (place(lax.rem(pos + 1, n)), place(lax.rem(pos + n - 1, n)))

    barrier = pltpu.get_barrier_semaphore()
    for other in (chan_up, chan_down) + ring:
        pl.semaphore_signal(barrier, inc=1, device_id={"chan": other}, device_id_type=MESH)
    for other in (band_up, band_down):
        pl.semaphore_signal(barrier, inc=1, device_id={"band": other}, device_id_type=MESH)

    lane = lax.broadcasted_iota(jnp.int32, (bins, lanes), 1)
    for k in range(2):
        for e in range(windows // per):
            last = first = jnp.zeros((bins, lanes), F32)
            for q in range(per):
                v = x_ref[k, e * per + q]
                here = (lane >= half * q) & (lane < half * (q + 1))
                last = jnp.where(here, rolled(v, half * (q + 1), 1), last)
                first = jnp.where(here, rolled(v, half * q, 1), first)
            edge_out[0, k, e] = last
            edge_out[1, k, e] = first
    pl.semaphore_wait(barrier, 6)

    edges = [
        pltpu.make_async_remote_copy(
            src_ref=edge_out.at[i], dst_ref=edge_in.at[i], send_sem=edge_send.at[i],
            recv_sem=edge_recv.at[i], device_id={"chan": other}, device_id_type=MESH,
        )
        for i, other in enumerate((chan_up, chan_down))
    ]
    for copy in edges:
        copy.start()

    mine = taps_ref[pl.ds(pl.multiple_of(group * bins, 8), bins), :]
    for t in range(tap_count):
        coef[t] = jnp.broadcast_to(mine[:, t : t + 1], (bins, lanes))
    for copy in edges:
        copy.wait_recv()

    sub = lax.broadcasted_iota(jnp.int32, (8, lanes), 0)

    def filter_group(g, carry):
        e = lax.div(g, per // 4)
        top = bottom = jnp.zeros((8, lanes), F32)
        for u in range(4):
            w = 4 * g + u
            start = half * (4 * lax.rem(g, per // 4) + u)
            done = []
            for k in range(2):
                v = x_ref[k, w]
                h = jnp.where(
                    lane < half,
                    pltpu.roll(edge_in[1, k, e], lax.rem(lanes - start, lanes), 1),
                    pltpu.roll(edge_in[0, k, e], lanes - half - start, 1),
                )
                total = jnp.zeros((bins, lanes), F32)
                for t in range(tap_count):
                    s = t - half
                    if s < 0:
                        src = jnp.where(lane >= lanes + s, h, v)
                    elif s > 0:
                        src = jnp.where(lane < s, h, v)
                    else:
                        src = v
                    total = total + coef[t] * rolled(src, -s, 1)
                filt[k, w] = total
                done.append(total)
            a = jnp.sqrt(done[0] * done[0] + done[1] * done[1])
            amp[w, 8 : 8 + bins] = a
            here = (sub >= 2 * u) & (sub < 2 * u + 2)
            top = jnp.where(here, rolled(a[bins - 8 :], 2 * u - 6, 0), top)
            bottom = jnp.where(here, rolled(a[:8], 2 * u, 0), bottom)
        rim_out[0, g] = top
        rim_out[1, g] = bottom
        return carry

    lax.fori_loop(0, groups, filter_group, 0)

    rims = [
        pltpu.make_async_remote_copy(
            src_ref=rim_out.at[i], dst_ref=rim_in.at[i], send_sem=rim_send.at[i],
            recv_sem=rim_recv.at[i], device_id={"band": other}, device_id_type=MESH,
        )
        for i, other in enumerate((band_up, band_down))
    ]
    for copy in rims:
        copy.start()
    for copy in rims:
        copy.wait_recv()

    keep_before = jnp.where(group == 0, 0.0, 1.0).astype(F32)
    keep_after = jnp.where(group == m - 1, 0.0, 1.0).astype(F32)

    def whiten_group(g, carry):
        before, after = rim_in[0, g] * keep_before, rim_in[1, g] * keep_after
        shown = ([], [])
        for u in range(4):
            w = 4 * g + u
            amp[w, 0:8] = rolled(before, 6 - 2 * u, 0)
            amp[w, 8 + bins : 16 + bins] = rolled(after, -2 * u, 0)
            total = jnp.zeros((bins, lanes), F32)
            for d in range(SMOOTH):
                total = total + amp[w, 6 + d : 6 + d + bins]
            inverse = 1.0 / (total * (1.0 / SMOOTH) + WATER)
            for k in range(2):
                shown[k].append(filt[k, w] * inverse)
        for k in range(2):
            low, mid, high = ([v[8 * i : 8 * i + 8] for v in shown[k]] for i in range(3))
            mixed = ([], [])
            for u in (0, 2):
                mixed[0].append(jnp.where(sub < 4, mid[u], rolled(mid[u + 1], 4, 0)))
                mixed[1].append(jnp.where(sub < 4, rolled(mid[u], 4, 0), mid[u + 1]))
            row = lax.div(g, groups // 2) * piece + k * part + lax.rem(g, groups // 2) * 48
            rows = pl.ds(pl.multiple_of(row, 16), 48)
            held[0, 0, rows, :] = jnp.concatenate(low + mixed[0], axis=0).astype(BF16)
            held[0, 1, rows, :] = jnp.concatenate(high + mixed[1], axis=0).astype(BF16)
        return carry

    def block(d, p, s):
        rows = pl.ds(p * piece, piece)
        return pltpu.make_async_remote_copy(
            src_ref=held.at[s, d, rows], dst_ref=held.at[s + 1, d, rows],
            send_sem=block_send.at[d, p, s], recv_sem=block_recv.at[d, p, s + 1],
            device_id={"chan": ring[d]}, device_id_type=MESH,
        )

    for p in range(2):
        lax.fori_loop(p * groups // 2, (p + 1) * groups // 2, whiten_group, 0)
        for d in range(2):
            block(d, p, 0).start()

    for b in range(2):
        own = held[0, b].astype(F32)
        turned = []
        for p in range(2):
            turned.append(own[p * piece + part : (p + 1) * piece])
            turned.append(-own[p * piece : p * piece + part])
        left[b, 0:lanes] = own.T.astype(BF16)
        left[b, lanes : 2 * lanes] = jnp.concatenate(turned, axis=0).T.astype(BF16)

    scale = 1.0 / (windows * BAND_BINS)

    def cross(s):
        for d in range(2):
            owner = place(lax.rem(pos + n - s if d == 0 else pos + s, n))
            columns = pl.ds(pl.multiple_of(owner * lanes, lanes), lanes)
            tile = jnp.dot(left[d], held[s, d], preferred_element_type=F32)
            tile = (tile * scale).astype(BF16)
            out_ref[d, 0, :, columns] = tile[:lanes]
            out_ref[d, 1, :, columns] = tile[lanes:]

    cross(0)

    def step(s, carry):
        for p in range(2):
            for d in range(2):
                block(d, p, s - 1).wait_recv()
                block(d, p, s).start()
        cross(s)
        return carry

    lax.fori_loop(1, n - 1, step, 0)
    for p in range(2):
        for d in range(2):
            block(d, p, n - 2).wait_recv()
    cross(n - 1)

    def drain(s, carry):
        for p in range(2):
            for d in range(2):
                block(d, p, s).wait_send()
        return carry

    lax.fori_loop(0, n - 1, drain, 0)
    for copy in edges + rims:
        copy.wait_send()


def body(n, m, spectra, taps):
    _, windows, bins, lanes = spectra.shape
    half = taps.shape[1] // 2
    per = lanes // half
    bands = bins // BAND_BINS
    depth = 2 * windows * BAND_BINS
    vmem = pl.BlockSpec(memory_space=pltpu.VMEM)
    dma = pltpu.SemaphoreType.DMA
    return pl.pallas_call(
        partial(kernel, n, m),
        out_shape=jax.ShapeDtypeStruct((bands, 2, lanes, n * lanes), BF16),
        in_specs=[vmem] * 2,
        out_specs=vmem,
        scratch_shapes=[
            pltpu.VMEM((taps.shape[1], bins, lanes), F32),
            pltpu.VMEM((2, 2, windows // per, bins, lanes), F32),
            pltpu.VMEM((2, 2, windows // per, bins, lanes), F32),
            pltpu.VMEM((2, windows, bins, lanes), F32),
            pltpu.VMEM((windows, bins + 16, lanes), F32),
            pltpu.VMEM((2, windows // 4, 8, lanes), F32),
            pltpu.VMEM((2, windows // 4, 8, lanes), F32),
            pltpu.VMEM((n, bands, depth, lanes), BF16),
            pltpu.VMEM((bands, 2 * lanes, depth), BF16),
            dma((2,)),
            dma((2,)),
            dma((2,)),
            dma((2,)),
            dma((2, 2, n)),
            dma((2, 2, n)),
        ],
        compiler_params=pltpu.CompilerParams(
            collective_id=0, has_side_effects=True, vmem_limit_bytes=56 * 2**20
        ),
    )(spectra, taps)


def solution(mesh):
    placed = (P(None, None, "band", "chan"), P())
    return jax.shard_map(
        partial(body, mesh.shape["chan"], mesh.shape["band"]),
        mesh=mesh, in_specs=placed, out_specs=P("band", None, "chan", None), check_vma=False,
    )
```

time: 112 us -> 58.3 us (0.52)
  the two profiles are of different devices: /device:TPU:0 before, /device:TPU:1 now
where the time goes in v1:
time: 58.3 us; the launch traced here: 57.7 us
  Pallas kernels  54 us (93%)
  local copies, waits for them, and re-layouts  3.67 us (6%)
    pallas_call x1, Pallas kernels, body(): pl.pallas_call(partial(kernel, n, m), out_shape=jax.ShapeDtypeStruct((ban...  54 us
    unnamed x2, local copies, waits for them, and re-layouts  3.67 us

profile of v1, /device:TPU:1, one launch (start us, length us, event | category | flops | bytes accessed | tf_op | source)
XLA Modules:
  0.0 57.7 jit_solution(15434165052941075477)
XLA Ops:
  0.0 1.4 %copy.3.taps_ref = f32[96,16]{1,0:T(8,128)} copy(f32[96,16]{0,1:T(8,128)} %param.3) | data formatting | bytes 12288 | tf_op args[1]
  1.4 54.0 %shard_map.28 = bf16[2,2,128,1024]{3,2,1,0:T(8,128)(2,1)} custom-call(f32[2,32,24,128]{3,2,1,0:T(8,128)} %x_ref.1, f32[96,16]{1,0:T(8,128)} %copy.3.taps_ref), custom_call_target="tpu_custom_call" | custom-call | tf_op jit(solution)/shard_map/pallas_call | solution.py:232
  55.5 2.3 %copy.5 = bf16[2,2,128,1024]{3,2,1,0:T(8,128)(2,1)} copy(bf16[2,2,128,1024]{3,2,1,0:T(8,128)(2,1)} %shard_map.28) | data formatting | bytes 2097152

commit v2 on v1

v2 whole, which is shorter than its diff:
```python
from functools import partial

import jax
import jax.numpy as jnp
from jax import lax
from jax.experimental import pallas as pl
from jax.experimental.pallas import tpu as pltpu
from jax.sharding import PartitionSpec as P

SMOOTH = 5
BAND_BINS = 12
WATER = 0.1
RETURNED = 3
PIECES = 4
MESH = pl.DeviceIdType.MESH
F32, BF16 = jnp.float32, jnp.bfloat16


def rolled(value, by, axis):
    if isinstance(by, int):
        by = by % value.shape[axis]
        if by == 0:
            return value
    return pltpu.roll(value, by, axis)


def kernel(
    n, m, bins, x_ref, taps_ref, out_ref, coef, taps_wide, turned_x, filt, amp, rim_out, rim_in, held, left,
    back_out, back_in, edge_send, edge_recv, rim_send, rim_recv, block_send, block_recv, back_send, back_recv,
):
    rows, lanes = x_ref.shape[1:]
    windows = rows // bins
    tap_count = taps_ref.shape[1]
    half = tap_count // 2
    groups = windows // 4
    depth = held.shape[2]
    piece = depth // PIECES
    part = piece // 2
    returned = back_in.shape[1]
    last = n - 1 - returned
    me = lax.axis_index("chan")
    group = lax.axis_index("band")
    chan_up, chan_down = lax.rem(me + 1, n), lax.rem(me + n - 1, n)
    band_up, band_down = lax.rem(group + 1, m), lax.rem(group + m - 1, m)
    odd = lax.rem(me, 2)
    pos = (1 - odd) * lax.div(me, 2) + odd * (n - 1 - lax.div(me, 2))

    def place(p):
        far = lax.div(p, (n + 1) // 2)
        return (1 - far) * 2 * p + far * (2 * (n - 1 - p) + 1)

    def at(d, s):
        return place(lax.rem(pos + s if d == 0 else pos + n - s, n))

    ring = (at(0, 1), at(1, 1))
    reached = [at(d, s) for s in range(1, max(1, returned) + 1) for d in range(2)]

    barrier = pltpu.get_barrier_semaphore()
    for other in [chan_up, chan_down] + reached:
        pl.semaphore_signal(barrier, inc=1, device_id={"chan": other}, device_id_type=MESH)
    for other in (band_up, band_down):
        pl.semaphore_signal(barrier, inc=1, device_id={"band": other}, device_id_type=MESH)

    for k in range(2):
        for j in range(0, rows, lanes):
            turned_x[k, half : half + lanes, j : j + lanes] = x_ref[k, j : j + lanes].T
    pl.semaphore_wait(barrier, len(reached) + 4)

    edges = [
        pltpu.make_async_remote_copy(
            src_ref=turned_x.at[:, pl.ds(src, half)], dst_ref=turned_x.at[:, pl.ds(dst, half)],
            send_sem=edge_send.at[i], recv_sem=edge_recv.at[i],
            device_id={"chan": other}, device_id_type=MESH,
        )
        for i, (other, src, dst) in enumerate(
            ((chan_up, lanes, 0), (chan_down, half, half + lanes))
        )
    ]
    for copy in edges:
        copy.start()

    mine = taps_ref[pl.ds(pl.multiple_of(group * bins, 8), bins), :]
    taps_wide[...] = jnp.zeros(taps_wide.shape, F32)
    taps_wide[:, 0:tap_count] = mine
    wide = taps_wide[...]
    coef[...] = jnp.concatenate([wide] * (windows // 2), axis=0).T[:tap_count]
    for copy in edges:
        copy.wait_recv()

    sub = lax.broadcasted_iota(jnp.int32, (8, lanes), 0)

    def filter_half(h):
        def tile(j, carry):
            here = pl.ds(pl.multiple_of(j * lanes, lanes), lanes)
            cols = pl.ds(pl.multiple_of(h * (rows // 2) + j * lanes, lanes), lanes)
            for k in range(2):
                done = []
                for r in range(0, lanes, lanes // 2):
                    total = jnp.zeros((lanes // 2, lanes), F32)
                    for t in range(tap_count):
                        total = total + coef[t : t + 1, here] * turned_x[k, r + t : r + t + lanes // 2, cols]
                    done.append(total)
                filt[k, cols, :] = jnp.concatenate(done, axis=0).T
            return carry

        lax.fori_loop(0, rows // 2 // lanes, tile, 0)

    def bins_of(w):
        return pl.ds(pl.multiple_of(w * bins, 8), bins)

    def amplitude_group(g, carry):
        top = bottom = jnp.zeros((8, lanes), F32)
        for u in range(4):
            w = 4 * g + u
            re, im = filt[0, bins_of(w), :], filt[1, bins_of(w), :]
            a = jnp.sqrt(re * re + im * im)
            amp[w, 8 : 8 + bins] = a
            here = (sub >= 2 * u) & (sub < 2 * u + 2)
            top = jnp.where(here, rolled(a[bins - 8 :], 2 * u - 6, 0), top)
            bottom = jnp.where(here, rolled(a[:8], 2 * u, 0), bottom)
        rim_out[0, g] = top
        rim_out[1, g] = bottom
        return carry

    rims = []
    for h in range(2):
        filter_half(h)
        lax.fori_loop(h * groups // 2, (h + 1) * groups // 2, amplitude_group, 0)
        some = pl.ds(h * groups // 2, groups // 2)
        rims.append(
            [
                pltpu.make_async_remote_copy(
                    src_ref=rim_out.at[i, some], dst_ref=rim_in.at[i, some],
                    send_sem=rim_send.at[i, h], recv_sem=rim_recv.at[i, h],
                    device_id={"band": other}, device_id_type=MESH,
                )
                for i, other in enumerate((band_up, band_down))
            ]
        )
        for copy in rims[h]:
            copy.start()

    keep_before = jnp.where(group == 0, 0.0, 1.0).astype(F32)
    keep_after = jnp.where(group == m - 1, 0.0, 1.0).astype(F32)

    def whiten_group(g, carry):
        before, after = rim_in[0, g] * keep_before, rim_in[1, g] * keep_after
        shown = ([], [])
        for u in range(4):
            w = 4 * g + u
            amp[w, 0:8] = rolled(before, 6 - 2 * u, 0)
            amp[w, 8 + bins : 16 + bins] = rolled(after, -2 * u, 0)
            total = jnp.zeros((bins, lanes), F32)
            for d in range(SMOOTH):
                total = total + amp[w, 6 + d : 6 + d + bins]
            inverse = 1.0 / (total * (1.0 / SMOOTH) + WATER)
            for k in range(2):
                shown[k].append(filt[k, bins_of(w), :] * inverse)
        for k in range(2):
            low, mid, high = ([v[8 * i : 8 * i + 8] for v in shown[k]] for i in range(3))
            mixed = ([], [])
            for u in (0, 2):
                mixed[0].append(jnp.where(sub < 4, mid[u], rolled(mid[u + 1], 4, 0)))
                mixed[1].append(jnp.where(sub < 4, rolled(mid[u], 4, 0), mid[u + 1]))
            row = lax.div(g, groups // PIECES) * piece + k * part + lax.rem(g, groups // PIECES) * 48
            chunk = pl.ds(pl.multiple_of(row, 16), 48)
            held[0, 0, chunk, :] = jnp.concatenate(low + mixed[0], axis=0).astype(BF16)
            held[0, 1, chunk, :] = jnp.concatenate(high + mixed[1], axis=0).astype(BF16)
        return carry

    def block(d, p, s):
        chunk = pl.ds(p * piece, piece)
        return pltpu.make_async_remote_copy(
            src_ref=held.at[s, d, chunk], dst_ref=held.at[s + 1, d, chunk],
            send_sem=block_send.at[d, p, s], recv_sem=block_recv.at[d, p, s + 1],
            device_id={"chan": ring[d]}, device_id_type=MESH,
        )

    for p in range(PIECES):
        if p % (PIECES // 2) == 0:
            for copy in rims[p // (PIECES // 2)]:
                copy.wait_recv()
        lax.fori_loop(p * groups // PIECES, (p + 1) * groups // PIECES, whiten_group, 0)
        for d in range(2):
            block(d, p, 0).start()

    for b in range(2):
        own = held[0, b].astype(F32)
        turned = []
        for p in range(PIECES):
            turned.append(own[p * piece + part : (p + 1) * piece])
            turned.append(-own[p * piece : p * piece + part])
        left[b, 0:lanes] = own.T.astype(BF16)
        left[b, lanes : 2 * lanes] = jnp.concatenate(turned, axis=0).T.astype(BF16)

    scale = 1.0 / (windows * BAND_BINS)

    def back(d, s):
        return pltpu.make_async_remote_copy(
            src_ref=back_out.at[d, s - 1], dst_ref=back_in.at[d, s - 1],
            send_sem=back_send.at[d, s - 1], recv_sem=back_recv.at[d, s - 1],
            device_id={"chan": at(1 - d, s)}, device_id_type=MESH,
        )

    def columns(owner):
        return pl.ds(pl.multiple_of(owner * lanes, lanes), lanes)

    def cross(s, send_back=False):
        for d in range(2):
            tile = jnp.dot(left[d], held[s, d], preferred_element_type=F32) * scale
            if send_back:
                back_out[d, s - 1, 0] = tile[:lanes].T.astype(BF16)
                back_out[d, s - 1, 1] = (-tile[lanes:]).T.astype(BF16)
                back(d, s).start()
            tile = tile.astype(BF16)
            here = columns(at(1 - d, s))
            out_ref[d, 0, :, here] = tile[:lanes]
            out_ref[d, 1, :, here] = tile[lanes:]

    cross(0)

    def step(s, carry, send_back=False):
        for p in range(PIECES):
            for d in range(2):
                block(d, p, s - 1).wait_recv()
                block(d, p, s).start()
        cross(s, send_back)
        return carry

    for s in range(1, returned + 1):
        step(s, 0, True)
    lax.fori_loop(returned + 1, last, step, 0)
    for p in range(PIECES):
        for d in range(2):
            block(d, p, last - 1).wait_recv()
    cross(last)
    for s in range(1, returned + 1):
        for d in range(2):
            back(d, s).wait_recv()
            here = columns(at(d, s))
            out_ref[d, 0, :, here] = back_in[d, s - 1, 0]
            out_ref[d, 1, :, here] = back_in[d, s - 1, 1]

    def drain(s, carry):
        for p in range(PIECES):
            for d in range(2):
                block(d, p, s).wait_send()
        return carry

    lax.fori_loop(0, last, drain, 0)
    for s in range(1, returned + 1):
        for d in range(2):
            back(d, s).wait_send()
    for copy in edges + rims[0] + rims[1]:
        copy.wait_send()


def body(n, m, spectra, taps):
    _, windows, bins, lanes = spectra.shape
    taps_count = taps.shape[1]
    returned = min(RETURNED, (n - 2) // 2)
    bands = bins // BAND_BINS
    depth = 2 * windows * BAND_BINS
    vmem = pl.BlockSpec(memory_space=pltpu.VMEM)
    dma = pltpu.SemaphoreType.DMA
    return pl.pallas_call(
        partial(kernel, n, m, bins),
        out_shape=jax.ShapeDtypeStruct((bands, 2, lanes, n * lanes), BF16),
        in_specs=[vmem] * 2,
        out_specs=vmem,
        scratch_shapes=[
            pltpu.VMEM((taps_count, windows * bins // 2), F32),
            pltpu.VMEM((bins, lanes), F32),
            pltpu.VMEM((2, lanes + taps_count, windows * bins), F32),
            pltpu.VMEM((2, windows * bins, lanes), F32),
            pltpu.VMEM((windows, bins + 16, lanes), F32),
            pltpu.VMEM((2, windows // 4, 8, lanes), F32),
            pltpu.VMEM((2, windows // 4, 8, lanes), F32),
            pltpu.VMEM((n - returned, bands, depth, lanes), BF16),
            pltpu.VMEM((bands, 2 * lanes, depth), BF16),
            pltpu.VMEM((2, returned, 2, lanes, lanes), BF16),
            pltpu.VMEM((2, returned, 2, lanes, lanes), BF16),
            dma((2,)),
            dma((2,)),
            dma((2, 2)),
            dma((2, 2)),
            dma((2, PIECES, n)),
            dma((2, PIECES, n)),
            dma((2, returned)),
            dma((2, returned)),
        ],
        compiler_params=pltpu.CompilerParams(
            collective_id=0, has_side_effects=True, vmem_limit_bytes=56 * 2**20
        ),
    )(spectra.reshape(2, windows * bins, lanes), taps)


def solution(mesh):
    placed = (P(None, None, "band", "chan"), P())
    return jax.shard_map(
        partial(body, mesh.shape["chan"], mesh.shape["band"]),
        mesh=mesh, in_specs=placed, out_specs=P("band", None, "chan", None), check_vma=False,
    )
```

time: 58.3 us -> 46.1 us (0.79)
  Pallas kernels: 54 us -> 42.1 us
    pallas_call x1, Pallas kernels: 54 us -> 42.1 us  [body(): pl.pallas_call(partial(kernel, n, m, bins), out_shape=jax.ShapeDtypeStruc...]
where the time goes in v2:
time: 46.1 us; the launch traced here: 45.8 us
  Pallas kernels  42.1 us (91%)
  local copies, waits for them, and re-layouts  3.67 us (8%)
    pallas_call x1, Pallas kernels, body(): pl.pallas_call(partial(kernel, n, m, bins), out_shape=jax.ShapeDtypeStruc...  42.1 us
    unnamed x2, local copies, waits for them, and re-layouts  3.67 us

profile of v2, /device:TPU:1, one launch (start us, length us, event | category | flops | bytes accessed | tf_op | source)
XLA Modules:
  0.0 45.8 jit_solution(10205285583864801000)
XLA Ops:
  0.0 1.4 %copy.3.taps_ref = f32[96,16]{1,0:T(8,128)} copy(f32[96,16]{0,1:T(8,128)} %param.3) | data formatting | bytes 12288 | tf_op args[1]
  1.4 42.1 %shard_map.28 = bf16[2,2,128,1024]{3,2,1,0:T(8,128)(2,1)} custom-call(f32[2,768,128]{2,1,0:T(8,128)} %bitcast.1, f32[96,16]{1,0:T(8,128)} %copy.3.taps_ref), custom_call_target="tpu_custom_call" | custom-call | tf_op jit(solution)/shard_map/pallas_call | solution.py:266
  43.6 2.3 %copy.5 = bf16[2,2,128,1024]{3,2,1,0:T(8,128)(2,1)} copy(bf16[2,2,128,1024]{3,2,1,0:T(8,128)(2,1)} %shard_map.28) | data formatting | bytes 2097152

commit v3 on v2

--- a/solution.py
+++ b/solution.py
@@ -25,12 +25,12 @@
 
 
 def kernel(
-    n, m, bins, x_ref, taps_ref, out_ref, coef, taps_wide, turned_x, filt, amp, rim_out, rim_in, held, left,
+    n, m, bins, x_hbm, taps_hbm, out_ref, x_ref, taps_ref, load_sem, coef, taps_wide, taps_turned, turned_x, mid, filt, amp, rim_out, rim_in, held, left,
     back_out, back_in, edge_send, edge_recv, rim_send, rim_recv, block_send, block_recv, back_send, back_recv,
 ):
     rows, lanes = x_ref.shape[1:]
     windows = rows // bins
-    tap_count = taps_ref.shape[1]
+    tap_count, all_bins = taps_ref.shape
     half = tap_count // 2
     groups = windows // 4
     depth = held.shape[2]
@@ -38,6 +38,11 @@
     part = piece // 2
     returned = back_in.shape[1]
     last = n - 1 - returned
+    loads = [
+        pltpu.make_async_copy(x_hbm.at[k], x_ref.at[k], load_sem.at[k]) for k in range(2)
+    ] + [pltpu.make_async_copy(taps_hbm, taps_ref, load_sem.at[2])]
+    for load in loads:
+        load.start()
     me = lax.axis_index("chan")
     group = lax.axis_index("band")
     chan_up, chan_down = lax.rem(me + 1, n), lax.rem(me + n - 1, n)
@@ -62,6 +67,7 @@
         pl.semaphore_signal(barrier, inc=1, device_id={"band": other}, device_id_type=MESH)
 
     for k in range(2):
+        loads[k].wait()
         for j in range(0, rows, lanes):
             turned_x[k, half : half + lanes, j : j + lanes] = x_ref[k, j : j + lanes].T
     pl.semaphore_wait(barrier, len(reached) + 4)
@@ -79,11 +85,32 @@
     for copy in edges:
         copy.start()
 
-    mine = taps_ref[pl.ds(pl.multiple_of(group * bins, 8), bins), :]
+    loads[2].wait()
     taps_wide[...] = jnp.zeros(taps_wide.shape, F32)
-    taps_wide[:, 0:tap_count] = mine
-    wide = taps_wide[...]
+    taps_wide[0:tap_count, 0:all_bins] = taps_ref[...]
+    taps_turned[...] = taps_wide[...].T
+    wide = taps_turned[pl.ds(pl.multiple_of(group * bins, 8), bins), :]
     coef[...] = jnp.concatenate([wide] * (windows // 2), axis=0).T[:tap_count]
+    def summed(k, start, count, here, cols):
+        total = jnp.zeros((count, lanes), F32)
+        for t in range(tap_count):
+            total = total + coef[t : t + 1, here] * turned_x[k, start + t : start + t + count, cols]
+        return total
+
+    def tile_of(j):
+        here = lax.rem(j, rows // 2 // lanes) * lanes
+        return pl.ds(pl.multiple_of(here, lanes), lanes), pl.ds(pl.multiple_of(j * lanes, lanes), lanes)
+
+    inner = lanes // 2 - half
+
+    def inner_tile(j, carry):
+        here, cols = tile_of(j)
+        for k in range(2):
+            for start in (half, half + inner):
+                mid[k, start : start + inner, cols] = summed(k, start, inner, here, cols)
+        return carry
+
+    lax.fori_loop(0, rows // lanes, inner_tile, 0)
     for copy in edges:
         copy.wait_recv()
 
@@ -91,19 +118,18 @@
 
     def filter_half(h):
         def tile(j, carry):
-            here = pl.ds(pl.multiple_of(j * lanes, lanes), lanes)
-            cols = pl.ds(pl.multiple_of(h * (rows // 2) + j * lanes, lanes), lanes)
+            here, cols = tile_of(j)
             for k in range(2):
-                done = []
-                for r in range(0, lanes, lanes // 2):
-                    total = jnp.zeros((lanes // 2, lanes), F32)
-                    for t in range(tap_count):
-                        total = total + coef[t : t + 1, here] * turned_x[k, r + t : r + t + lanes // 2, cols]
-                    done.append(total)
-                filt[k, cols, :] = jnp.concatenate(done, axis=0).T
+                parts = [
+                    summed(k, 0, half, here, cols),
+                    mid[k, half : lanes - half, cols],
+                    summed(k, lanes - half, half, here, cols),
+                ]
+                filt[k, cols, :] = jnp.concatenate(parts, axis=0).T
             return carry
 
-        lax.fori_loop(0, rows // 2 // lanes, tile, 0)
+        tiles = rows // lanes
+        lax.fori_loop(h * tiles // 2, (h + 1) * tiles // 2, tile, 0)
 
     def bins_of(w):
         return pl.ds(pl.multiple_of(w * bins, 8), bins)
@@ -259,6 +285,7 @@
     _, windows, bins, lanes = spectra.shape
     taps_count = taps.shape[1]
     returned = min(RETURNED, (n - 2) // 2)
+    wide = pl.cdiv(taps.shape[0], lanes) * lanes
     bands = bins // BAND_BINS
     depth = 2 * windows * BAND_BINS
     vmem = pl.BlockSpec(memory_space=pltpu.VMEM)
@@ -266,12 +293,17 @@
     return pl.pallas_call(
         partial(kernel, n, m, bins),
         out_shape=jax.ShapeDtypeStruct((bands, 2, lanes, n * lanes), BF16),
-        in_specs=[vmem] * 2,
+        in_specs=[pl.BlockSpec(memory_space=pltpu.HBM)] * 2,
         out_specs=vmem,
         scratch_shapes=[
+            pltpu.VMEM((2, windows * bins, lanes), F32),
+            pltpu.VMEM(taps.shape[::-1], F32),
+            dma((3,)),
             pltpu.VMEM((taps_count, windows * bins // 2), F32),
-            pltpu.VMEM((bins, lanes), F32),
+            pltpu.VMEM((lanes, wide), F32),
+            pltpu.VMEM((wide, lanes), F32),
             pltpu.VMEM((2, lanes + taps_count, windows * bins), F32),
+            pltpu.VMEM((2, lanes, windows * bins), F32),
             pltpu.VMEM((2, windows * bins, lanes), F32),
             pltpu.VMEM((windows, bins + 16, lanes), F32),
             pltpu.VMEM((2, windows // 4, 8, lanes), F32),
@@ -292,7 +324,7 @@
         compiler_params=pltpu.CompilerParams(
             collective_id=0, has_side_effects=True, vmem_limit_bytes=56 * 2**20
         ),
-    )(spectra.reshape(2, windows * bins, lanes), taps)
+    )(spectra.reshape(2, windows * bins, lanes), taps.T)
 
 
 def solution(mesh):

time: 46.1 us -> 42.7 us (0.926)
  Pallas kernels: 42.1 us -> 40.3 us
  local copies, waits for them, and re-layouts: 3.67 us -> 2.26 us
    pallas_call x1, Pallas kernels: 42.1 us -> 40.3 us  [body(): pl.pallas_call(partial(kernel, n, m, bins), out_shape=jax.ShapeDtypeStruc...]
    unnamed x2 -> x1, local copies, waits for them, and re-layouts: 3.67 us -> 2.26 us
where the time goes in v3:
time: 42.7 us; the launch traced here: 42.6 us
  Pallas kernels  40.3 us (94%)
  local copies, waits for them, and re-layouts  2.26 us (5%)
    pallas_call x1, Pallas kernels, body(): pl.pallas_call(partial(kernel, n, m, bins), out_shape=jax.ShapeDtypeStruc...  40.3 us
    unnamed x1, local copies, waits for them, and re-layouts  2.26 us

profile of v3, /device:TPU:1, one launch (start us, length us, event | category | flops | bytes accessed | tf_op | source)
XLA Modules:
  0.0 42.6 jit_solution(14740098136136888319)
XLA Ops:
  0.0 40.3 %shard_map.28 = bf16[2,2,128,1024]{3,2,1,0:T(8,128)(2,1)} custom-call(f32[2,768,128]{2,1,0:T(8,128)} %bitcast.2, f32[16,96]{1,0:T(8,128)} %bitcast.3), custom_call_target="tpu_custom_call" | custom-call | tf_op jit(solution)/shard_map/pallas_call | solution.py:293
  40.3 2.3 %copy.4 = bf16[2,2,128,1024]{3,2,1,0:T(8,128)(2,1)} copy(bf16[2,2,128,1024]{3,2,1,0:T(8,128)(2,1)} %shard_map.28) | data formatting | bytes 2097152

commit v4 on v3

--- a/solution.py
+++ b/solution.py
@@ -110,7 +110,7 @@
                 mid[k, start : start + inner, cols] = summed(k, start, inner, here, cols)
         return carry
 
-    lax.fori_loop(0, rows // lanes, inner_tile, 0)
+    lax.fori_loop(0, rows // lanes, inner_tile, 0, unroll=True)
     for copy in edges:
         copy.wait_recv()
 
@@ -129,7 +129,7 @@
             return carry
 
         tiles = rows // lanes
-        lax.fori_loop(h * tiles // 2, (h + 1) * tiles // 2, tile, 0)
+        lax.fori_loop(h * tiles // 2, (h + 1) * tiles // 2, tile, 0, unroll=True)
 
     def bins_of(w):
         return pl.ds(pl.multiple_of(w * bins, 8), bins)
@@ -151,7 +151,7 @@
     rims = []
     for h in range(2):
         filter_half(h)
-        lax.fori_loop(h * groups // 2, (h + 1) * groups // 2, amplitude_group, 0)
+        lax.fori_loop(h * groups // 2, (h + 1) * groups // 2, amplitude_group, 0, unroll=True)
         some = pl.ds(h * groups // 2, groups // 2)
         rims.append(
             [
@@ -206,7 +206,7 @@
         if p % (PIECES // 2) == 0:
             for copy in rims[p // (PIECES // 2)]:
                 copy.wait_recv()
-        lax.fori_loop(p * groups // PIECES, (p + 1) * groups // PIECES, whiten_group, 0)
+        lax.fori_loop(p * groups // PIECES, (p + 1) * groups // PIECES, whiten_group, 0, unroll=True)
         for d in range(2):
             block(d, p, 0).start()
 

time: 42.7 us -> 42.5 us (level)
  no operation moved by 1% of the time
where the time goes in v4:
time: 42.5 us; the launch traced here: 42.3 us
  Pallas kernels  40 us (94%)
  local copies, waits for them, and re-layouts  2.26 us (5%)
    pallas_call x1, Pallas kernels, body(): pl.pallas_call(partial(kernel, n, m, bins), out_shape=jax.ShapeDtypeStruc...  40 us
    unnamed x1, local copies, waits for them, and re-layouts  2.26 us

profile of v4, /device:TPU:1, one launch (start us, length us, event | category | flops | bytes accessed | tf_op | source)
XLA Modules:
  0.0 42.3 jit_solution(10553770637827655162)
XLA Ops:
  0.0 40.0 %shard_map.28 = bf16[2,2,128,1024]{3,2,1,0:T(8,128)(2,1)} custom-call(f32[2,768,128]{2,1,0:T(8,128)} %bitcast.2, f32[16,96]{1,0:T(8,128)} %bitcast.3), custom_call_target="tpu_custom_call" | custom-call | tf_op jit(solution)/shard_map/pallas_call | solution.py:293
  40.0 2.3 %copy.4 = bf16[2,2,128,1024]{3,2,1,0:T(8,128)(2,1)} copy(bf16[2,2,128,1024]{3,2,1,0:T(8,128)(2,1)} %shard_map.28) | data formatting | bytes 2097152
